TPU v7x, 512 devices: a whole 4x8x8 slice. The times are simulated.
512 devices in a mesh: enc: 32 (over y, x_hi, core), seq: 16 (over z, x_lo).
Axes of the slice: x: 4 (x_hi: 2, x_lo: 2; x = x_hi * 2 + x_lo), y: 8, z: 8, core: 2. Of those that a mesh axis runs over, the one named last changes fastest.
Arguments:
- tile_features: bfloat16 [32, 256, 2560], P('enc', 'seq'), may hold values from -6 to 6
- proj_weight: bfloat16 [2560, 4096], P(None, 'seq'), may hold values from -0.125 to 0.125
- text_embed: bfloat16 [32, 2048, 4096], P('enc', 'seq'), may hold values from -8 to 8
- out_grad: bfloat16 [32, 2048, 4096], P('enc', 'seq'), may hold values from -6 to 6
- score_gain: float32 [4096], P('seq'), may hold values from -6 to 6
- tile_count: int32 [32], P('enc'), may hold values from 0 to 1, as said below
- tile_slot: int32 [32, 1], P('enc'), may hold values from 0 to 7, as said below
- doc_id: int32 [32, 2048], P('enc'), may hold values from 0 to 7, never falling along the last dimension, each value on 1 to 1024 neighbouring positions
Outputs:
- text_grad: bfloat16 [32, 2048, 4096], P('enc', 'seq')
- weight_grad: float32 [2560, 4096], P('enc', 'seq')
Inputs may be any that keep to these rules, and one draw needn't show every extreme that they name: `tile_count`: in every draw some sequence has 1 tiles. `tile_slot`: the 1 entries of a sequence are different slots; slot j covers positions j * 256 to j * 256 + 255; only the first tile_count entries are used.
All inputs are finite; a program needn't handle non-finite values.
Results may differ from a plain program's by a relative error of at most 0.013.
The roundings to bfloat16 on the way count: a program that leaves them out, or rounds other values in their place, can miss the bound.
Values may be sent and summed in bfloat16 or wider, within the bound.
A program may use at most 128 MiB of HBM per device.

v0:
```python
import jax
import jax.numpy as jnp
from jax import lax
from jax.sharding import PartitionSpec as P

HEAD = 128
TILE_TOK = 256


def head_grads(emb_head, gain_head, cot_head, doc_row):
    length = emb_head.shape[0]
    head_width = emb_head.shape[1]
    block_rows = min(512, length)
    scaling = head_width ** (-0.5)
    queries = (emb_head.astype(jnp.float32) * gain_head).astype(jnp.bfloat16)
    position = jnp.arange(length, dtype=jnp.int32)
    key_terms = jnp.zeros((length, head_width), jnp.float32)
    query_terms = []
    for row_first in range(0, length, block_rows):
        row_last = row_first + block_rows
        key_rows = emb_head[:row_last]
        query_rows = queries[row_first:row_last]
        cot_rows = cot_head[row_first:row_last]
        allowed = (position[None, :row_last] <= position[row_first:row_last, None]) & (
            doc_row[None, :row_last] == doc_row[row_first:row_last, None]
        )
        scores = jnp.dot(query_rows, key_rows.T, preferred_element_type=jnp.float32) * scaling
        scores = jnp.where(allowed, scores, jnp.float32(-1e30))
        row_max = jnp.max(scores, axis=1, keepdims=True)
        weights = jnp.where(allowed, jnp.exp(scores - row_max), jnp.float32(0.0))
        prob_rows = weights / jnp.sum(weights, axis=1, keepdims=True)
        prob_low = prob_rows.astype(jnp.bfloat16)
        d_prob = jnp.dot(cot_rows, key_rows.T, preferred_element_type=jnp.float32)
        row_term = jnp.sum(prob_rows * d_prob, axis=1, keepdims=True)
        d_scores = (prob_rows * (d_prob - row_term) * scaling).astype(jnp.bfloat16)
        query_terms.append(jnp.dot(d_scores, key_rows, preferred_element_type=jnp.float32))
        block_term = jnp.dot(d_scores.T, query_rows, preferred_element_type=jnp.float32) + jnp.dot(
            prob_low.T, cot_rows, preferred_element_type=jnp.float32
        )
        key_terms = key_terms.at[:row_last].add(block_term)
    return jnp.concatenate(query_terms, axis=0) * gain_head + key_terms


def per_device(
    tile_features, proj_weight, text_embed, out_grad, score_gain, tile_count, tile_slot, doc_id
):
    features = lax.all_gather(tile_features[0], "seq", axis=0, tiled=True)
    projected = jnp.dot(features, proj_weight, preferred_element_type=jnp.float32).astype(
        jnp.bfloat16
    )
    columns = proj_weight.shape[1]
    length = doc_id.shape[1]
    rows_dev = text_embed.shape[1]
    slot_count = length // TILE_TOK
    tile_max = tile_slot.shape[1]
    live_tiles = jnp.arange(tile_max, dtype=jnp.int32) < tile_count[0]
    choose = (
        tile_slot[0][None, :] == jnp.arange(slot_count, dtype=jnp.int32)[:, None]
    ) & live_tiles[None, :]
    choose_low = choose.astype(jnp.bfloat16)
    placed = (
        jnp.dot(
            choose_low,
            projected.reshape(tile_max, TILE_TOK * columns),
            preferred_element_type=jnp.float32,
        )
        .astype(jnp.bfloat16)
        .reshape(length, columns)
    )
    is_image = jnp.repeat(jnp.any(choose, axis=1), TILE_TOK)
    arrived_rows = lax.all_to_all(placed, "seq", split_axis=0, concat_axis=1, tiled=True)
    own_rows = lax.dynamic_slice_in_dim(is_image, lax.axis_index("seq") * rows_dev, rows_dev)
    outgoing = jnp.where(own_rows[:, None], arrived_rows, text_embed[0])
    arrived, cotangent = (
        lax.all_to_all(outgoing, "seq", split_axis=1, concat_axis=0, tiled=True),
        lax.all_to_all(out_grad[0], "seq", split_axis=1, concat_axis=0, tiled=True),
    )
    doc_row = doc_id[0]

    def one_head(head_index, gradient):
        offset = head_index * HEAD
        result = head_grads(
            lax.dynamic_slice_in_dim(arrived, offset, HEAD, 1),
            lax.dynamic_slice_in_dim(score_gain, offset, HEAD, 0),
            lax.dynamic_slice_in_dim(cotangent, offset, HEAD, 1),
            doc_row,
        )
        return lax.dynamic_update_slice_in_dim(gradient, result, offset, 1)

    gradient = lax.fori_loop(
        0, columns // HEAD, one_head, jnp.zeros((length, columns), jnp.float32)
    )
    grad_low = gradient.astype(jnp.bfloat16)
    text_heads = jnp.where(is_image[:, None], jnp.zeros_like(grad_low), grad_low)
    text_grad = lax.all_to_all(text_heads, "seq", split_axis=0, concat_axis=1, tiled=True)
    image_grad = (
        jnp.dot(
            choose_low.T,
            grad_low.reshape(slot_count, TILE_TOK * columns),
            preferred_element_type=jnp.float32,
        )
        .astype(jnp.bfloat16)
        .reshape(tile_max * TILE_TOK, columns)
    )
    weight_grad = lax.psum_scatter(
        lax.dot_general(
            features, image_grad, (((0,), (0,)), ((), ())), preferred_element_type=jnp.float32
        ),
        "enc",
        scatter_dimension=0,
        tiled=True,
    ) * (1.0 / TILE_TOK)
    return (text_grad[None], weight_grad)


def solution(mesh):
    in_specs = (
        P("enc", "seq", None),
        P(None, "seq"),
        P("enc", "seq", None),
        P("enc", "seq", None),
        P("seq"),
        P("enc"),
        P("enc", None),
        P("enc", None),
    )
    out_specs = (P("enc", "seq", None), P("enc", "seq"))
    return jax.shard_map(
        per_device, mesh=mesh, in_specs=in_specs, out_specs=out_specs, check_vma=False
    )
```

profile of v0, /device:TPU:1, one launch (start us, length us, event | category | flops | bytes accessed | tf_op | source)
XLA Modules:
  0.0 352.2 jit_solution(12273580935558751486)
XLA Ops:
  7.2 0.7 all-gather.3.cloned.1.call-update
  9.2 69.4 %all-gather.3.cloned.1.call-done = bf16[1,256,2560]{2,1,0:T(8,128)(2,1)} async-done(((bf16[1,16,2560]{2,1,0:T(8,128)(2,1)}), bf16[1,256,2560]{2,1,0:T(8,128)(2,1)}) %all-gather.3.cloned.1.call-update) | async-done | bytes 1310736 | tf_op jit(solution)/shard_map/all_gather | solution.py:47
  78.6 1.8 fusion.89
  80.8 1.4 all_to_all.50
  82.2 6.1 %all-to-all-start = ((bf16[16,128,256]{2,1,0:T(8,128)(2,1)}), bf16[16,128,256]{2,1,0:T(8,128)(2,1)S(1)}, u32[]{:S(2)}, u32[]{:S(2)}) async-start(bf16[16,128,256]{2,1,0:T(8,128)(2,1)} %all_to_all.50), calls=%async_computation | async-start | bytes 2097152 | tf_op jit(solution)/shard_map/all_to_all | solution.py:71
  88.6 1.3 copy.18
  89.9 15.6 %all-to-all-done = bf16[16,128,256]{2,1,0:T(8,128)(2,1)S(1)} async-done(((bf16[16,128,256]{2,1,0:T(8,128)(2,1)}), bf16[16,128,256]{2,1,0:T(8,128)(2,1)S(1)}, u32[]{:S(2)}, u32[]{:S(2)}) %all-to-all-start) | async-done | bytes 1048608 | tf_op jit(solution)/shard_map/all_to_all | solution.py:71
  105.5 6.6 %all-to-all-start.2 = ((bf16[128,16,256]{2,0,1:T(8,128)(2,1)}), bf16[128,16,256]{2,0,1:T(8,128)(2,1)S(1)}, u32[]{:S(2)}, u32[]{:S(2)}) async-start(bf16[128,16,256]{2,0,1:T(8,128)(2,1)} %copy.18), calls=%async_computation.2 | async-start | bytes 2097152 | tf_op jit(solution)/shard_map/all_to_all | solution.py:76
  112.2 1.5 copy.25
  113.8 1.3 bitcast_select_fusion
  115.1 15.7 %all-to-all-done.2 = bf16[128,16,256]{2,0,1:T(8,128)(2,1)S(1)} async-done(((bf16[128,16,256]{2,0,1:T(8,128)(2,1)}), bf16[128,16,256]{2,0,1:T(8,128)(2,1)S(1)}, u32[]{:S(2)}, u32[]{:S(2)}) %all-to-all-start.2) | async-done | bytes 1048608 | tf_op jit(solution)/shard_map/all_to_all | solution.py:76
  130.8 5.9 %all-to-all-start.1 = ((bf16[128,16,256]{2,0,1:T(8,128)(2,1)}), bf16[128,16,256]{2,0,1:T(8,128)(2,1)S(1)}, u32[]{:S(2)}, u32[]{:S(2)}) async-start(bf16[128,16,256]{2,0,1:T(8,128)(2,1)} %bitcast_select_fusion), calls=%async_computation.1 | async-start | bytes 2097152 | tf_op jit(solution)/shard_map/all_to_all | solution.py:75
  136.8 18.7 %all-to-all-done.1 = bf16[128,16,256]{2,0,1:T(8,128)(2,1)S(1)} async-done(((bf16[128,16,256]{2,0,1:T(8,128)(2,1)}), bf16[128,16,256]{2,0,1:T(8,128)(2,1)S(1)}, u32[]{:S(2)}, u32[]{:S(2)}) %all-to-all-start.1) | async-done | bytes 1048608 | tf_op jit(solution)/shard_map/all_to_all | solution.py:75
  155.6 43.0 %while.29 = (s32[]{:T(128)}, bf16[2048,256]{1,0:T(8,128)(2,1)S(1)}, s32[2048]{0:T(1024)S(1)}, bf16[2048,256]{1,0:T(8,128)(2,1)S(1)}, f32[256]{0:T(256)S(1)}, /*i...) while((s32[]{:T(128)}, bf16[2048,256]{1,0:T(8,128)(2,1)S(1)}, ...), condition=%wide.region_13.14_spmd, body=%wide.region_0.13_spmd.sunk | while | flops 3433757184 | bytes 119557392 | solution.py:90
  158.9 0.7 fusion.182
  159.6 0.8 fusion.183
  160.5 1.0 multiply_reduce_fusion.9
  163.3 1.0 fusion.186
  164.3 1.0 fusion.187
  165.3 1.3 multiply_reduce_fusion.10
  168.2 0.7 fusion.189
  168.9 1.3 fusion.190
  170.3 1.8 fusion.191
  172.1 2.0 multiply_reduce_fusion.11
  174.6 0.7 fusion.193
  175.4 0.7 fusion.192
  176.1 1.0 fusion.197
  180.2 0.7 fusion.182
  180.9 0.8 fusion.183
  181.8 1.0 multiply_reduce_fusion.9
  184.6 1.0 fusion.186
  185.6 1.0 fusion.187
  186.6 1.3 multiply_reduce_fusion.10
  189.5 0.7 fusion.189
  190.2 1.3 fusion.190
  191.6 1.8 fusion.191
  193.4 2.0 multiply_reduce_fusion.11
  195.9 0.7 fusion.193
  196.7 0.7 fusion.192
  197.4 1.0 fusion.197
  199.6 1.8 convolution_bitcast_fusion
  201.5 2.1 copy.22
  203.6 1.2 copy-done.3
  205.3 27.5 %all_to_all.67 = bf16[16,128,256]{2,1,0:T(8,128)(2,1)S(1)} all-to-all(bf16[16,128,256]{2,1,0:T(8,128)(2,1)S(1)} %bitcast.79), channel_id=1, replica_groups=mesh['enc'=32,'seq'=16] {'seq'}, dimensions={0} | all-to-all | bytes 2097152 | tf_op jit(solution)/shard_map/all_to_all | solution.py:95
  233.4 1.3 copy.20
  234.8 108.9 %reduce-scatter.4.cloned.1.call-done = f32[80,256]{1,0:T(8,128)} async-done(((f32[2560,256]{1,0:T(8,128)}), f32[80,256]{1,0:T(8,128)}) %reduce-scatter.4.cloned.1.call-update) | async-done | bytes 81936
  343.7 1.0 copy.23
  344.7 0.7 copy.21
  (86 shorter events, 16.9 us)
Async XLA Ops:
  7.2 71.4 %copy-start = (bf16[2560,256]{1,0:T(8,128)(2,1)S(1)}, bf16[2560,256]{1,0:T(8,128)(2,1)}, u32[]{:S(2)}) copy-start(bf16[2560,256]{1,0:T(8,128)(2,1)} %param.21) | copy-start | bytes 3932164
  7.2 71.4 %all-gather.3.cloned.1.call-start = ((), (), s32[]{:S(2)}) async-start(), calls=%async_computation.5 | async-start | bytes 1392640 | tf_op jit(solution)/shard_map/all_gather | solution.py:47
  80.4 7.9 %copy-start.5 = (bf16[1,128,4096]{2,1,0:T(8,128)(2,1)S(1)}, bf16[1,128,4096]{2,1,0:T(8,128)(2,1)}, u32[]{:S(2)}) copy-start(bf16[1,128,4096]{2,1,0:T(8,128)(2,1)} %param.23) | copy-start | bytes 3145732
  82.2 23.3 %all-to-all-start = ((bf16[16,128,256]{2,1,0:T(8,128)(2,1)}), bf16[16,128,256]{2,1,0:T(8,128)(2,1)S(1)}, u32[]{:S(2)}, u32[]{:S(2)}) async-start(bf16[16,128,256]{2,1,0:T(8,128)(2,1)} %all_to_all.50), calls=%async_computation | async-start | bytes 2097152 | tf_op jit(solution)/shard_map/all_to_all | solution.py:71
  105.5 25.3 %all-to-all-start.2 = ((bf16[128,16,256]{2,0,1:T(8,128)(2,1)}), bf16[128,16,256]{2,0,1:T(8,128)(2,1)S(1)}, u32[]{:S(2)}, u32[]{:S(2)}) async-start(bf16[128,16,256]{2,0,1:T(8,128)(2,1)} %copy.18), calls=%async_computation.2 | async-start | bytes 2097152 | tf_op jit(solution)/shard_map/all_to_all | solution.py:76
  112.2 1.6 copy-start.6
  113.8 41.8 %copy-start.4 = (s32[1,2048]{1,0:T(1,128)S(1)}, s32[1,2048]{1,0:T(1,128)}, u32[]{:S(2)}) copy-start(s32[1,2048]{1,0:T(1,128)} %param.27) | copy-start | bytes 24580
  113.8 41.9 %copy-start.8 = (f32[256]{0:T(256)S(1)}, f32[256]{0:T(256)}, u32[]{:S(2)}) copy-start(f32[256]{0:T(256)} %param.24) | copy-start | bytes 3076
  130.8 24.7 %all-to-all-start.1 = ((bf16[128,16,256]{2,0,1:T(8,128)(2,1)}), bf16[128,16,256]{2,0,1:T(8,128)(2,1)S(1)}, u32[]{:S(2)}, u32[]{:S(2)}) async-start(bf16[128,16,256]{2,0,1:T(8,128)(2,1)} %bitcast_select_fusion), calls=%async_computation.1 | async-start | bytes 2097152 | tf_op jit(solution)/shard_map/all_to_all | solution.py:75
  136.7 206.9 %reduce-scatter.4.cloned.1.call-start = ((), (), s32[]{:S(2)}) async-start(), calls=%async_computation.6 | async-start | bytes 2703360
  198.6 1.0 copy-start.2
  201.5 2.1 copy-start.7
  203.6 1.2 copy-start.3
  205.3 140.1 %copy-start.1 = (bf16[2560,256]{1,0:T(8,128)(2,1)S(1)}, bf16[2560,256]{1,0:T(8,128)(2,1)}, u32[]{:S(2)}) copy-start(bf16[2560,256]{1,0:T(8,128)(2,1)} %param.21) | copy-start | bytes 3932164
Sparse Core Ops, SparseCore 0:
  10.1 68.4 all-gather.2
  203.8 139.8 reduce-scatter.3
where the time goes:
time: 357 us; the launch traced here: 352 us
  waiting for transfers between devices  229 us (64%)
  matrix products  34.4 us (10%)
  blocking collectives  27.5 us (8%)
  starting transfers between devices  18.7 us (5%)
  between operations  15.6 us (4%)
  other arithmetic  13.7 us (4%)
  local copies, waits for them, and re-layouts  12.8 us (4%)
    unnamed x3, waiting for transfers between devices  110 us
    all_gather x1, waiting for transfers between devices, per_device(): features = lax.all_gather(tile_features[0], 'seq', axis=0, tiled=True)  69.4 us
    all_to_all x1, blocking collectives, per_device(): lax.all_to_all(text_heads, 'seq', split_axis=0, concat_axis=1, tiled=True)  27.5 us
    all_to_all x1, waiting for transfers between devices, per_device(): lax.all_to_all(outgoing, 'seq', split_axis=1, concat_axis=0, tiled=True)  18.7 us
    all_to_all x1, waiting for transfers between devices, per_device(): lax.all_to_all(out_grad[0], 'seq', split_axis=1, concat_axis=0, tiled=True)  15.7 us
    all_to_all x1, waiting for transfers between devices, per_device(): lax.all_to_all(placed, 'seq', split_axis=0, concat_axis=1, tiled=True)  15.6 us
    dot_general x8, matrix products, head_grads(): d_prob = jnp.dot(cot_rows, key_rows.T, preferred_element_type=jnp.float32)  9.62 us
    unnamed x25, local copies, waits for them, and re-layouts  8.24 us
  transfers between devices with their start and end apart: 5, of which 5 were waited for; matrix products, arithmetic and copies ran while one was open for 2% of the time, Pallas kernels for 0%

commit v1 on v0

v1 whole, which is shorter than its diff:
```python
import functools

import jax
import jax.numpy as jnp
from jax import lax
from jax.experimental import pallas as pl
from jax.experimental.pallas import tpu as pltpu
from jax.sharding import PartitionSpec as P

HEAD = 128
TILE_TOK = 256
BLOCK = 128
REACH = 1024
DOC_VALUES = 8
NEG = -1e30
MESH = pl.DeviceIdType.MESH
F32 = jnp.float32
BF16 = jnp.bfloat16


def whole_kernel(
    n,
    heads,
    enc,
    feat,
    weight,
    text,
    cot,
    gain,
    count,
    slot,
    doc,
    out,
    wgrad,
    features,
    featT,
    wv,
    projected,
    tx,
    qc,
    emb,
    embT,
    dkv,
    pair,
    image,
    send_block,
    first,
    keep,
    half_out,
    half_in,
    sum_out,
    sum_in,
    local_sem,
    gather_send,
    gather_recv,
    in_send,
    in_recv,
    grad_send,
    grad_recv,
    half_send,
    half_recv,
    sum_send,
    sum_recv,
    block_sem,
):
    me = lax.axis_index("seq")
    my_enc = lax.axis_index("enc")
    core = lax.rem(my_enc, 2)
    chip = lax.div(my_enc, 2)
    chips = enc // 2
    other_core = my_enc + 1 - 2 * core
    beside = me + 1 - 2 * lax.rem(me, 2)
    columns = heads * HEAD
    shard = feat.shape[1]
    depth = feat.shape[2]
    length = n * BLOCK
    out_rows = depth // enc
    peers = n - 1

    def seq_id(index):
        return (my_enc, index)

    def along(step):
        return lax.rem(me + 2 * step + 2 * n, n)

    def rows(index, size):
        return pl.ds(pl.multiple_of(index * size, size), size)

    weight_copy = pltpu.make_async_copy(weight, wv, local_sem.at[0])
    weight_copy.start()
    own_features = pltpu.make_async_copy(
        feat.at[0], features.at[rows(me, shard)], local_sem.at[1]
    )
    own_features.start()
    own = []
    for h in range(heads):
        cols = pl.ds(pl.multiple_of(me * columns + h * HEAD, HEAD), HEAD)
        own.append(
            pltpu.make_async_copy(
                text.at[0, :, cols], tx.at[h, rows(me, BLOCK)], local_sem.at[2 + 2 * h]
            )
        )
        own.append(
            pltpu.make_async_copy(
                cot.at[0, :, cols],
                qc.at[h, me, pl.ds(BLOCK, BLOCK)],
                local_sem.at[3 + 2 * h],
            )
        )
    for copy in own:
        copy.start()

    barrier = pltpu.get_barrier_semaphore()

    def greet_seq(d, carry):
        pl.semaphore_signal(
            barrier, inc=1, device_id=seq_id(lax.rem(me + d, n)), device_id_type=MESH
        )
        return carry

    def greet_enc(d, carry):
        to = 2 * lax.rem(chip + d, chips) + core
        pl.semaphore_signal(barrier, inc=1, device_id=(to, me), device_id_type=MESH)
        return carry

    lax.fori_loop(1, n, greet_seq, 0)
    lax.fori_loop(1, chips, greet_enc, 0)
    pl.semaphore_signal(barrier, inc=1, device_id=(other_core, me), device_id_type=MESH)
    pl.semaphore_wait(barrier, peers + chips)

    def pass_on(source, index, to, number, first_col=0, cols=depth):
        span = pl.ds(first_col, cols)
        place = features.at[rows(index, shard), span]
        return pltpu.make_async_remote_copy(
            src_ref=place if source is None else source,
            dst_ref=place,
            send_sem=gather_send.at[number],
            recv_sem=gather_recv.at[number],
            device_id=seq_id(to),
            device_id_type=MESH,
        )

    ring = n // 2
    ahead, behind = along(1), along(-1)
    full_steps = ring // 2 - 1
    half = depth // 2

    def exchange(h, source, to_cot, begin, end):
        def body(d, carry):
            to = lax.rem(me + d, n)
            cols = pl.ds(pl.multiple_of(to * columns + h * HEAD, HEAD), HEAD)
            if to_cot:
                place = qc.at[h, me, pl.ds(BLOCK, BLOCK)]
            else:
                place = tx.at[h, rows(me, BLOCK)]
            pltpu.make_async_remote_copy(
                src_ref=source.at[0, :, cols],
                dst_ref=place,
                send_sem=in_send.at[2 * h + to_cot],
                recv_sem=in_recv.at[2 * h + to_cot],
                device_id=seq_id(to),
                device_id_type=MESH,
            ).start()
            return carry

        lax.fori_loop(begin, end, body, 0)

    def exchange_part(h, part, parts):
        begin = 1 + peers * part // parts
        end = 1 + peers * (part + 1) // parts
        exchange(h, text, 0, begin, end)
        exchange(h, cot, 1, begin, end)

    x_base = 2 * (full_steps + 1)
    copies = []
    parts = full_steps + 1
    for step in range(full_steps):
        if step == 0:
            source = feat.at[0]
            right = pass_on(source, me, ahead, 0)
            left = pass_on(source, me, behind, full_steps + 1)
            sideways = [pass_on(source, me, beside, x_base)]
        else:
            copies[-1][0].wait_recv()
            right = pass_on(None, along(-step), ahead, step)
            copies[-1][1].wait_recv()
            left = pass_on(None, along(step), behind, full_steps + 1 + step)
            sideways = [
                pass_on(None, along(-step), beside, x_base + 2 * step - 1),
                pass_on(None, along(step), beside, x_base + 2 * step),
            ]
        for copy in [right, left] + sideways:
            copy.start()
        copies.append([right, left] + sideways)
        exchange_part(0, step, parts)
    copies[-1][0].wait_recv()
    copies[-1][1].wait_recv()
    last = full_steps
    right = pass_on(None, along(-last), ahead, last, 0, half)
    left = pass_on(None, along(last), behind, full_steps + 1 + last, half, half)
    sideways = [
        pass_on(None, along(-last), beside, x_base + 2 * last - 1),
        pass_on(None, along(last), beside, x_base + 2 * last),
    ]
    for copy in [right, left] + sideways:
        copy.start()
    exchange_part(0, parts - 1, parts)
    right.wait_recv()
    left.wait_recv()
    farthest = pass_on(None, along(ring // 2), beside, x_base + 2 * last + 1)
    farthest.start()
    copies.append([right, left] + sideways + [farthest])

    for h in range(1, heads):
        exchange_part(h, 0, 1)

    doc_row = doc[...]
    begins = jnp.zeros_like(doc_row)
    for value in range(1, DOC_VALUES):
        below = jnp.sum((doc_row < value).astype(jnp.int32), axis=1, keepdims=True)
        begins = jnp.where(doc_row >= value, below, begins)
    first[...] = begins
    tile = jnp.where(count[0] > 0, slot[0, 0], -1)

    for group in copies:
        for copy in group[2:]:
            copy.wait_recv()
    own_features.wait()
    weight_copy.wait()

    projected[...] = jnp.dot(
        features[...], wv[...], preferred_element_type=F32
    ).astype(BF16)

    def turn_features(index, carry):
        place = rows(index, HEAD)
        featT[place, :] = features[:, place].T
        return carry

    lax.fori_loop(0, depth // HEAD, turn_features, 0)
    for copy in own:
        copy.wait()

    scaling = HEAD ** (-0.5)
    log2_scaling = scaling * 1.4426950408889634
    tile_blocks = TILE_TOK // BLOCK

    def of_tile(block):
        return jnp.full((BLOCK, HEAD), tile, jnp.int32) == lax.div(block, tile_blocks)

    def await_blocks(like, sem):
        pltpu.make_async_copy(like, like, sem).wait()

    def one_head(h, head_carry):
        head_cols = rows(h, HEAD)
        gain_row = gain[:, head_cols]
        arrived = tx.at[h, pl.ds(0, peers * BLOCK)]
        await_blocks(arrived, in_recv.at[2 * h])
        await_blocks(arrived, in_recv.at[2 * h + 1])

        def prepare(block, carry):
            place = rows(block, BLOCK)
            part = rows(lax.rem(block, tile_blocks), BLOCK)
            value = jnp.where(
                of_tile(block),
                projected[part, head_cols].astype(F32),
                tx[h, place, :].astype(F32),
            )
            low = value.astype(BF16)
            emb[place, :] = low
            embT[:, place] = value.T.astype(BF16)
            qc[h, block, 0:BLOCK, :] = (value * gain_row).astype(BF16)
            return carry

        lax.fori_loop(0, n, prepare, 0)
        dkv[...] = jnp.zeros_like(dkv)
        image[...] = jnp.zeros_like(image)

        def attend(block, base, width, plain):
            band = pl.ds(base, width)
            here = rows(block, BLOCK)
            both = qc[h, block]
            products = lax.dot_general(
                emb[band, :], both, (((1,), (1,)), ((), ())), preferred_element_type=F32
            )
            start = first[:, here] - base
            lane = lax.broadcasted_iota(jnp.int32, (BLOCK, BLOCK), 1) + (
                block * BLOCK - base
            )
            row = lax.broadcasted_iota(jnp.int32, (BLOCK, BLOCK), 0)
            scores = []
            for at in range(0, width, BLOCK):
                allowed = row + at >= start
                if at >= plain:
                    allowed = allowed & (row + at <= lane)
                scores.append(
                    jnp.where(allowed, products[at : at + BLOCK, :BLOCK], NEG)
                )
            highest = scores[0]
            for part in scores[1:]:
                highest = jnp.maximum(highest, part)
            highest = jnp.max(highest, axis=0, keepdims=True)
            total = jnp.zeros((BLOCK, BLOCK), F32)
            weighted = jnp.zeros((BLOCK, BLOCK), F32)
            weights = []
            for index, part in enumerate(scores):
                at = index * BLOCK
                value = jnp.exp2((part - highest) * log2_scaling)
                weights.append(value)
                total = total + value
                weighted = weighted + value * products[at : at + BLOCK, BLOCK:]
            share = 1.0 / jnp.sum(total, axis=0, keepdims=True)
            row_term = jnp.sum(weighted, axis=0, keepdims=True) * share
            scaled_share = share * scaling
            for index, value in enumerate(weights):
                at = index * BLOCK
                change = value * (products[at : at + BLOCK, BLOCK:] - row_term)
                pair[at : at + BLOCK, :BLOCK] = (change * scaled_share).astype(BF16)
                pair[at : at + BLOCK, BLOCK:] = (value * share).astype(BF16)
            dkv[band, :] += jnp.dot(
                pair[0:width, :], both, preferred_element_type=F32
            )
            queryT = jnp.dot(
                embT[:, band], pair[0:width, :BLOCK], preferred_element_type=F32
            )
            grad = queryT.T * gain_row + dkv[here, :]
            low = grad.astype(BF16).astype(F32)
            tile_here = of_tile(block)
            send_block[h, block] = jnp.where(tile_here, 0.0, low).astype(BF16)
            part = rows(lax.rem(block, tile_blocks), BLOCK)
            image[part, :] = jnp.where(
                tile_here, low, image[part, :].astype(F32)
            ).astype(BF16)

            target = out.at[
                0,
                :,
                pl.ds(pl.multiple_of(me * columns + h * HEAD, HEAD), HEAD),
            ]

            @pl.when(block == me)
            def _():
                pltpu.make_async_copy(
                    send_block.at[h, block], target, block_sem.at[h]
                ).start()

            @pl.when(block != me)
            def _():
                pltpu.make_async_remote_copy(
                    src_ref=send_block.at[h, block],
                    dst_ref=target,
                    send_sem=grad_send.at[h],
                    recv_sem=grad_recv.at[h],
                    device_id=seq_id(block),
                    device_id_type=MESH,
                ).start()

        reach = REACH // BLOCK

        def far(step, carry):
            block = n - 1 - step
            base = pl.multiple_of((block - reach) * BLOCK, BLOCK)
            attend(block, base, (reach + 1) * BLOCK, reach * BLOCK)
            return carry

        def near(high, low):
            def body(step, carry):
                attend(high - 1 - step, 0, high * BLOCK, low * BLOCK)
                return carry

            lax.fori_loop(0, high - low, body, 0)

        lax.fori_loop(0, n - reach, far, 0)
        near(reach, reach // 2)
        near(reach // 2, 0)

        tile_grad = image[...]

        def weight_rows(index, carry):
            mine = pl.multiple_of((2 * index + core) * out_rows, out_rows)
            theirs = pl.multiple_of((2 * index + 1 - core) * out_rows, out_rows)
            half_out[h, index] = jnp.dot(
                featT[pl.ds(theirs, out_rows), :],
                tile_grad,
                preferred_element_type=F32,
            ).astype(BF16)
            keep[index] = jnp.dot(
                featT[pl.ds(mine, out_rows), :],
                tile_grad,
                preferred_element_type=F32,
            )
            return carry

        lax.fori_loop(0, chips, weight_rows, 0)
        halves = pltpu.make_async_remote_copy(
            src_ref=half_out.at[h],
            dst_ref=half_in.at[h],
            send_sem=half_send.at[h],
            recv_sem=half_recv.at[h],
            device_id=(other_core, me),
            device_id_type=MESH,
        )
        halves.start()
        halves.wait()

        def add_halves(index, carry):
            value = keep[index] + half_in[h, index].astype(F32)
            keep[index] = value
            sum_out[h, index] = value.astype(BF16)
            return carry

        lax.fori_loop(0, chips, add_halves, 0)
        wgrad[:, head_cols] = keep[chip]

        def send_sums(d, carry):
            to = lax.rem(chip + d, chips)
            pltpu.make_async_remote_copy(
                src_ref=sum_out.at[h, to],
                dst_ref=sum_in.at[h, d - 1],
                send_sem=sum_send.at[h],
                recv_sem=sum_recv.at[h],
                device_id=(2 * to + core, me),
                device_id_type=MESH,
            ).start()
            return carry

        lax.fori_loop(1, chips, send_sums, 0)
        return head_carry

    lax.fori_loop(0, heads, one_head, 0)

    def finish(h, carry):
        head_cols = rows(h, HEAD)
        await_blocks(sum_in.at[h], sum_recv.at[h])
        total = wgrad[:, head_cols]
        for d in range(chips - 1):
            total = total + sum_in[h, d].astype(F32)
        wgrad[:, head_cols] = total * (1.0 / TILE_TOK)
        return carry

    lax.fori_loop(0, heads, finish, 0)

    for h in range(heads):
        sent = tx.at[h, pl.ds(0, peers * BLOCK)]
        await_blocks(sent, in_send.at[2 * h])
        await_blocks(sent, in_send.at[2 * h + 1])
        await_blocks(sum_in.at[h], sum_send.at[h])
        await_blocks(sent, grad_send.at[h])
        await_blocks(sent, grad_recv.at[h])
        pltpu.make_async_copy(
            send_block.at[h, 0], send_block.at[h, 0], block_sem.at[h]
        ).wait()
    for group in copies:
        for copy in group:
            copy.wait_send()


def per_device(
    n, enc, feat, weight, text, cot, gain, count, slot, doc
):
    heads = weight.shape[1] // HEAD
    depth = weight.shape[0]
    length = doc.shape[1]
    chips = enc // 2
    out_rows = depth // enc
    tile_rows = feat.shape[1] * n
    anywhere = pl.BlockSpec(memory_space=pl.ANY)
    vmem = pl.BlockSpec(memory_space=pltpu.VMEM)
    smem = pl.BlockSpec(memory_space=pltpu.SMEM)
    dma = pltpu.SemaphoreType.DMA
    ring_copies = 2 * (n // 4) + n // 2 + 2
    return pl.pallas_call(
        functools.partial(whole_kernel, n, heads, enc),
        out_shape=(
            jax.ShapeDtypeStruct(text.shape, BF16),
            jax.ShapeDtypeStruct((out_rows, heads * HEAD), F32),
        ),
        in_specs=[anywhere] * 4 + [vmem, smem, smem, vmem],
        out_specs=(anywhere, vmem),
        scratch_shapes=[
            pltpu.VMEM((tile_rows, depth), BF16),
            pltpu.VMEM((depth, tile_rows), BF16),
            pltpu.VMEM((depth, heads * HEAD), BF16),
            pltpu.VMEM((tile_rows, heads * HEAD), BF16),
            pltpu.VMEM((heads, length, HEAD), BF16),
            pltpu.VMEM((heads, n, 2 * BLOCK, HEAD), BF16),
            pltpu.VMEM((length, HEAD), BF16),
            pltpu.VMEM((HEAD, length), BF16),
            pltpu.VMEM((length, HEAD), F32),
            pltpu.VMEM((REACH + BLOCK, 2 * BLOCK), BF16),
            pltpu.VMEM((tile_rows, HEAD), BF16),
            pltpu.VMEM((heads, n, BLOCK, HEAD), BF16),
            pltpu.VMEM((1, length), jnp.int32),
            pltpu.VMEM((chips, out_rows, HEAD), F32),
            pltpu.VMEM((heads, chips, out_rows, HEAD), BF16),
            pltpu.VMEM((heads, chips, out_rows, HEAD), BF16),
            pltpu.VMEM((heads, chips, out_rows, HEAD), BF16),
            pltpu.VMEM((heads, chips - 1, out_rows, HEAD), BF16),
            dma((2 + 2 * heads,)),
            dma((ring_copies,)),
            dma((ring_copies,)),
            dma((2 * heads,)),
            dma((2 * heads,)),
            dma((heads,)),
            dma((heads,)),
            dma((heads,)),
            dma((heads,)),
            dma((heads,)),
            dma((heads,)),
            dma((heads,)),
        ],
        compiler_params=pltpu.CompilerParams(
            collective_id=0, has_side_effects=True, vmem_limit_bytes=48 * 2**20
        ),
    )(feat, weight, text, cot, gain.reshape(1, -1), count, slot, doc)


def solution(mesh):
    in_specs = (
        P("enc", "seq", None),
        P(None, "seq"),
        P("enc", "seq", None),
        P("enc", "seq", None),
        P("seq"),
        P("enc"),
        P("enc", None),
        P("enc", None),
    )
    out_specs = (P("enc", "seq", None), P("enc", "seq"))
    return jax.shard_map(
        functools.partial(per_device, mesh.shape["seq"], mesh.shape["enc"]),
        mesh=mesh,
        in_specs=in_specs,
        out_specs=out_specs,
        check_vma=False,
    )
```

time: 357 us -> 132 us (0.37)
  waiting for transfers between devices: 229 us -> 0 us
  Pallas kernels: 0 us -> 121 us
  matrix products: 34.4 us -> 0 us
  blocking collectives: 27.5 us -> 0 us
  starting transfers between devices: 18.7 us -> 0 us
  other arithmetic: 13.7 us -> 0 us
  between operations: 15.6 us -> 1.95 us
  local copies, waits for them, and re-layouts: 12.8 us -> 7.63 us
    pallas_call x0 -> x1, Pallas kernels: none -> 121 us  [per_device(): pl.pallas_call(functools.partial(whole_kernel, n, heads, enc), out_shape=...]
    unnamed x3 -> x0, waiting for transfers between devices: 110 us -> none
    all_gather x1 -> x0, waiting for transfers between devices: 69.4 us -> none  [per_device(): features = lax.all_gather(tile_features[0], 'seq', axis=0, tiled=True)]
    all_to_all x3 -> x0, waiting for transfers between devices: 50 us -> none  [the longest x1 18.7 us: per_device(): lax.all_to_all(outgoing, 'seq', split_axis=1, concat_axis=0, tiled=True)]
    dot_general x43 -> x0, matrix products: 34.4 us -> none  [the longest x8 9.62 us: head_grads(): d_prob = jnp.dot(cot_rows, key_rows.T, preferred_element_type=jnp.float32)]
    all_to_all x1 -> x0, blocking collectives: 27.5 us -> none  [per_device(): lax.all_to_all(text_heads, 'seq', split_axis=0, concat_axis=1, tiled=True)]
    all_to_all x3 -> x0, starting transfers between devices: 18.6 us -> none  [the longest x1 6.56 us: per_device(): lax.all_to_all(out_grad[0], 'seq', split_axis=1, concat_axis=0, tiled=True)]
    reduce_sum x8 -> x0, other arithmetic: 7.93 us -> none  [head_grads(): prob_rows = weights / jnp.sum(weights, axis=1, keepdims=True)]
  transfers between devices with their start and end apart: 5 -> 0, of which waited for: 5 -> 0; matrix products, arithmetic and copies ran while one was open for 2% -> 0% of each run, Pallas kernels for 0% -> 0%
where the time goes in v1:
time: 132 us; the launch traced here: 130 us
  Pallas kernels  121 us (92%)
  local copies, waits for them, and re-layouts  7.63 us (6%)
  between operations  1.95 us (1%)
    pallas_call x1, Pallas kernels, per_device(): pl.pallas_call(functools.partial(whole_kernel, n, heads, enc), out_shape=...  121 us
    unnamed x14, local copies, waits for them, and re-layouts  7.63 us

profile of v1, /device:TPU:1, one launch (start us, length us, event | category | flops | bytes accessed | tf_op | source)
XLA Modules:
  0.0 130.2 jit_solution(5788193541375410066)
XLA Ops:
  1.9 0.0 copy-start
  1.9 1.3 %copy-done = bf16[2560,256]{1,0:T(8,128)(2,1)S(1)} copy-done((bf16[2560,256]{1,0:T(8,128)(2,1)S(1)}, bf16[2560,256]{1,0:T(8,128)(2,1)}, u32[]{:S(2)}) %copy-start) | copy-done | bytes 1310744
  3.2 0.0 copy-start.1
  3.2 1.2 copy-done.1
  4.5 0.0 copy-start.2
  4.5 1.2 copy-done.2
  5.7 0.0 copy-start.3
  5.7 0.9 copy-done.3
  6.6 0.0 copy-start.4
  6.6 0.7 copy-done.4
  7.3 0.0 copy-start.5
  7.3 0.7 copy-done.5
  8.0 120.6 %shard_map.95 = (bf16[1,128,4096]{2,1,0:T(8,128)(2,1)S(1)}, f32[80,256]{1,0:T(8,128)S(1)}) custom-call(bf16[1,16,2560]{2,1,0:T(8,128)(2,1)S(1)} %copy-done.3, bf16[2560,256]{1,0:T(8,128)(2,1)S(1)} %copy-done, bf16[1,128,4096]{2,1,0:T(8,128)(2,1)S(1)} %copy-done.1, bf16[1,128,4096]{2,1,0:T(8,128)(2,1)S(1)} %copy-done.2, f32[1,256]{1,0:T(1,128)S(1)} %bitcast.1, ...), custom_call_target="tpu_custom_call" | custom-call | tf_op jit(solution)/shard_map/pallas_call | solution.py:472
  128.6 1.0 copy.14
  129.6 0.6 copy.15
Async XLA Ops:
  1.9 1.3 %copy-start = (bf16[2560,256]{1,0:T(8,128)(2,1)S(1)}, bf16[2560,256]{1,0:T(8,128)(2,1)}, u32[]{:S(2)}) copy-start(bf16[2560,256]{1,0:T(8,128)(2,1)} %weight.1) | copy-start | bytes 3932164
  3.2 1.2 copy-start.1
  4.5 1.2 copy-start.2
  5.7 0.9 copy-start.3
  6.6 0.7 copy-start.4
  7.3 0.7 copy-start.5

commit v2 on v1

--- a/solution.py
+++ b/solution.py
@@ -10,9 +10,11 @@
 HEAD = 128
 TILE_TOK = 256
 BLOCK = 128
+GROUP = 256
 REACH = 1024
 DOC_VALUES = 8
 NEG = -1e30
+NT = (((1,), (1,)), ((), ()))
 MESH = pl.DeviceIdType.MESH
 F32 = jnp.float32
 BF16 = jnp.bfloat16
@@ -26,10 +28,10 @@
     weight,
     text,
     cot,
-    gain,
+    gain_in,
     count,
     slot,
-    doc,
+    doc_in,
     out,
     wgrad,
     features,
@@ -37,13 +39,17 @@
     wv,
     projected,
     tx,
-    qc,
+    ct,
+    queries,
     emb,
     embT,
     dkv,
-    pair,
+    d_scores,
+    probs,
     image,
     send_block,
+    gain,
+    doc,
     first,
     keep,
     half_out,
@@ -103,12 +109,16 @@
         own.append(
             pltpu.make_async_copy(
                 cot.at[0, :, cols],
-                qc.at[h, me, pl.ds(BLOCK, BLOCK)],
+                ct.at[h, rows(me, BLOCK)],
                 local_sem.at[3 + 2 * h],
             )
         )
     for copy in own:
         copy.start()
+    gain_copy = pltpu.make_async_copy(gain_in, gain, local_sem.at[2 + 2 * heads])
+    gain_copy.start()
+    doc_copy = pltpu.make_async_copy(doc_in, doc, local_sem.at[3 + 2 * heads])
+    doc_copy.start()
 
     barrier = pltpu.get_barrier_semaphore()
 
@@ -149,10 +159,7 @@
         def body(d, carry):
             to = lax.rem(me + d, n)
             cols = pl.ds(pl.multiple_of(to * columns + h * HEAD, HEAD), HEAD)
-            if to_cot:
-                place = qc.at[h, me, pl.ds(BLOCK, BLOCK)]
-            else:
-                place = tx.at[h, rows(me, BLOCK)]
+            place = (ct if to_cot else tx).at[h, rows(me, BLOCK)]
             pltpu.make_async_remote_copy(
                 src_ref=source.at[0, :, cols],
                 dst_ref=place,
@@ -214,6 +221,8 @@
     for h in range(1, heads):
         exchange_part(h, 0, 1)
 
+    doc_copy.wait()
+    gain_copy.wait()
     doc_row = doc[...]
     begins = jnp.zeros_like(doc_row)
     for value in range(1, DOC_VALUES):
@@ -243,137 +252,127 @@
 
     scaling = HEAD ** (-0.5)
     log2_scaling = scaling * 1.4426950408889634
-    tile_blocks = TILE_TOK // BLOCK
-
-    def of_tile(block):
-        return jnp.full((BLOCK, HEAD), tile, jnp.int32) == lax.div(block, tile_blocks)
+    groups = length // GROUP
+    group_reach = REACH // GROUP
 
     def await_blocks(like, sem):
         pltpu.make_async_copy(like, like, sem).wait()
 
-    def one_head(h, head_carry):
-        head_cols = rows(h, HEAD)
-        gain_row = gain[:, head_cols]
-        arrived = tx.at[h, pl.ds(0, peers * BLOCK)]
-        await_blocks(arrived, in_recv.at[2 * h])
-        await_blocks(arrived, in_recv.at[2 * h + 1])
-
-        def prepare(block, carry):
-            place = rows(block, BLOCK)
-            part = rows(lax.rem(block, tile_blocks), BLOCK)
+    def prepare(h, gain_row):
+        def body(index, carry):
+            place = rows(index, GROUP)
+            of_tile = jnp.full((GROUP, HEAD), tile, jnp.int32) == index
             value = jnp.where(
-                of_tile(block),
-                projected[part, head_cols].astype(F32),
+                of_tile,
+                projected[:, h * HEAD : (h + 1) * HEAD].astype(F32),
                 tx[h, place, :].astype(F32),
             )
             low = value.astype(BF16)
             emb[place, :] = low
-            embT[:, place] = value.T.astype(BF16)
-            qc[h, block, 0:BLOCK, :] = (value * gain_row).astype(BF16)
+            embT[:, place] = low.T
+            queries[place, :] = (value * gain_row).astype(BF16)
             return carry
 
-        lax.fori_loop(0, n, prepare, 0)
+        lax.fori_loop(0, groups, body, 0)
+
+    def score_part(h, index):
+        least = max(0, index - group_reach)
+        base, parts = least * GROUP, index + 1 - least
+        here = pl.ds(index * GROUP, GROUP)
+        query, cotangent = queries[here, :], ct[h, here, :]
+        start = first[:, here] - base
+        row = lax.broadcasted_iota(jnp.int32, (GROUP, GROUP), 0)
+        lane = lax.broadcasted_iota(jnp.int32, (GROUP, GROUP), 1)
+        scores, d_probs = [], []
+        for part in range(parts):
+            keys = emb[pl.ds(base + part * GROUP, GROUP), :]
+            score = lax.dot_general(keys, query, NT, preferred_element_type=F32)
+            d_probs.append(
+                lax.dot_general(keys, cotangent, NT, preferred_element_type=F32)
+            )
+            allowed = row >= start - part * GROUP
+            if part == parts - 1:
+                allowed = allowed & (row <= lane)
+            scores.append(jnp.where(allowed, score, NEG))
+        highest = jnp.max(scores[0], axis=0, keepdims=True)
+        for score in scores[1:]:
+            highest = jnp.maximum(highest, jnp.max(score, axis=0, keepdims=True))
+        total = jnp.zeros((1, GROUP), F32)
+        weighted = jnp.zeros((1, GROUP), F32)
+        weights = []
+        for score, d_prob in zip(scores, d_probs):
+            value = jnp.exp2((score - highest) * log2_scaling)
+            weights.append(value)
+            total = total + jnp.sum(value, axis=0, keepdims=True)
+            weighted = weighted + jnp.sum(value * d_prob, axis=0, keepdims=True)
+        share = 1.0 / total
+        row_term = weighted * share
+        scaled_share = share * scaling
+        turn = index % 2
+        for part, (value, d_prob) in enumerate(zip(weights, d_probs)):
+            place = pl.ds(part * GROUP, GROUP)
+            change = value * (d_prob - row_term)
+            d_scores[turn, place, :] = (change * scaled_share).astype(BF16)
+            probs[turn, place, :] = (value * share).astype(BF16)
+
+    def product_part(h, index, gain_row):
+        least = max(0, index - group_reach)
+        width = (index + 1 - least) * GROUP
+        band, here = pl.ds(least * GROUP, width), pl.ds(index * GROUP, GROUP)
+        d_score = d_scores[index % 2, 0:width, :]
+        dkv[band, :] += jnp.dot(
+            d_score, queries[here, :], preferred_element_type=F32
+        ) + jnp.dot(
+            probs[index % 2, 0:width, :], ct[h, here, :], preferred_element_type=F32
+        )
+        queryT = jnp.dot(embT[:, band], d_score, preferred_element_type=F32)
+        grad = queryT.T * gain_row + dkv[here, :]
+        low = grad.astype(BF16).astype(F32)
+        of_tile = jnp.full((GROUP, HEAD), tile, jnp.int32) == index
+        send_block[h, here, :] = jnp.where(of_tile, 0.0, low).astype(BF16)
+        image[...] = jnp.where(of_tile, low, image[...].astype(F32)).astype(BF16)
+
+    def send_grad(h, block):
+        source = send_block.at[h, rows(block, BLOCK)]
+        target = out.at[
+            0, :, pl.ds(pl.multiple_of(me * columns + h * HEAD, HEAD), HEAD)
+        ]
+
+        @pl.when(me == block)
+        def _():
+            pltpu.make_async_copy(source, target, block_sem.at[h]).start()
+
+        @pl.when(me != block)
+        def _():
+            pltpu.make_async_remote_copy(
+                src_ref=source,
+                dst_ref=target,
+                send_sem=grad_send.at[h],
+                recv_sem=grad_recv.at[h],
+                device_id=seq_id(block),
+                device_id_type=MESH,
+            ).start()
+
+    def send_grads(h, begin, end):
+        def body(step, carry):
+            send_grad(h, end - 1 - step)
+            return carry
+
+        lax.fori_loop(0, end - begin, body, 0)
+
+    def attend(h, gain_row, at_once):
         dkv[...] = jnp.zeros_like(dkv)
         image[...] = jnp.zeros_like(image)
-
-        def attend(block, base, width, plain):
-            band = pl.ds(base, width)
-            here = rows(block, BLOCK)
-            both = qc[h, block]
-            products = lax.dot_general(
-                emb[band, :], both, (((1,), (1,)), ((), ())), preferred_element_type=F32
-            )
-            start = first[:, here] - base
-            lane = lax.broadcasted_iota(jnp.int32, (BLOCK, BLOCK), 1) + (
-                block * BLOCK - base
-            )
-            row = lax.broadcasted_iota(jnp.int32, (BLOCK, BLOCK), 0)
-            scores = []
-            for at in range(0, width, BLOCK):
-                allowed = row + at >= start
-                if at >= plain:
-                    allowed = allowed & (row + at <= lane)
-                scores.append(
-                    jnp.where(allowed, products[at : at + BLOCK, :BLOCK], NEG)
-                )
-            highest = scores[0]
-            for part in scores[1:]:
-                highest = jnp.maximum(highest, part)
-            highest = jnp.max(highest, axis=0, keepdims=True)
-            total = jnp.zeros((BLOCK, BLOCK), F32)
-            weighted = jnp.zeros((BLOCK, BLOCK), F32)
-            weights = []
-            for index, part in enumerate(scores):
-                at = index * BLOCK
-                value = jnp.exp2((part - highest) * log2_scaling)
-                weights.append(value)
-                total = total + value
-                weighted = weighted + value * products[at : at + BLOCK, BLOCK:]
-            share = 1.0 / jnp.sum(total, axis=0, keepdims=True)
-            row_term = jnp.sum(weighted, axis=0, keepdims=True) * share
-            scaled_share = share * scaling
-            for index, value in enumerate(weights):
-                at = index * BLOCK
-                change = value * (products[at : at + BLOCK, BLOCK:] - row_term)
-                pair[at : at + BLOCK, :BLOCK] = (change * scaled_share).astype(BF16)
-                pair[at : at + BLOCK, BLOCK:] = (value * share).astype(BF16)
-            dkv[band, :] += jnp.dot(
-                pair[0:width, :], both, preferred_element_type=F32
-            )
-            queryT = jnp.dot(
-                embT[:, band], pair[0:width, :BLOCK], preferred_element_type=F32
-            )
-            grad = queryT.T * gain_row + dkv[here, :]
-            low = grad.astype(BF16).astype(F32)
-            tile_here = of_tile(block)
-            send_block[h, block] = jnp.where(tile_here, 0.0, low).astype(BF16)
-            part = rows(lax.rem(block, tile_blocks), BLOCK)
-            image[part, :] = jnp.where(
-                tile_here, low, image[part, :].astype(F32)
-            ).astype(BF16)
-
-            target = out.at[
-                0,
-                :,
-                pl.ds(pl.multiple_of(me * columns + h * HEAD, HEAD), HEAD),
-            ]
-
-            @pl.when(block == me)
-            def _():
-                pltpu.make_async_copy(
-                    send_block.at[h, block], target, block_sem.at[h]
-                ).start()
-
-            @pl.when(block != me)
-            def _():
-                pltpu.make_async_remote_copy(
-                    src_ref=send_block.at[h, block],
-                    dst_ref=target,
-                    send_sem=grad_send.at[h],
-                    recv_sem=grad_recv.at[h],
-                    device_id=seq_id(block),
-                    device_id_type=MESH,
-                ).start()
-
-        reach = REACH // BLOCK
-
-        def far(step, carry):
-            block = n - 1 - step
-            base = pl.multiple_of((block - reach) * BLOCK, BLOCK)
-            attend(block, base, (reach + 1) * BLOCK, reach * BLOCK)
-            return carry
-
-        def near(high, low):
-            def body(step, carry):
-                attend(high - 1 - step, 0, high * BLOCK, low * BLOCK)
-                return carry
-
-            lax.fori_loop(0, high - low, body, 0)
-
-        lax.fori_loop(0, n - reach, far, 0)
-        near(reach, reach // 2)
-        near(reach // 2, 0)
-
+        blocks = GROUP // BLOCK
+        for index in range(groups - 1, -2, -1):
+            if index >= 0:
+                score_part(h, index)
+            if index < groups - 1:
+                product_part(h, index + 1, gain_row)
+                if at_once:
+                    send_grads(h, (index + 1) * blocks, (index + 2) * blocks)
+
+    def weight_term(h):
         tile_grad = image[...]
 
         def weight_rows(index, carry):
@@ -401,6 +400,9 @@
             device_id_type=MESH,
         )
         halves.start()
+        return halves
+
+    def send_sums(h, halves):
         halves.wait()
 
         def add_halves(index, carry):
@@ -410,9 +412,9 @@
             return carry
 
         lax.fori_loop(0, chips, add_halves, 0)
-        wgrad[:, head_cols] = keep[chip]
-
-        def send_sums(d, carry):
+        wgrad[:, h * HEAD : (h + 1) * HEAD] = keep[chip]
+
+        def body(d, carry):
             to = lax.rem(chip + d, chips)
             pltpu.make_async_remote_copy(
                 src_ref=sum_out.at[h, to],
@@ -424,21 +426,30 @@
             ).start()
             return carry
 
-        lax.fori_loop(1, chips, send_sums, 0)
-        return head_carry
-
-    lax.fori_loop(0, heads, one_head, 0)
-
-    def finish(h, carry):
-        head_cols = rows(h, HEAD)
+        lax.fori_loop(1, chips, body, 0)
+
+    def finish(h):
+        cols = slice(h * HEAD, (h + 1) * HEAD)
         await_blocks(sum_in.at[h], sum_recv.at[h])
-        total = wgrad[:, head_cols]
+        total = wgrad[:, cols]
         for d in range(chips - 1):
             total = total + sum_in[h, d].astype(F32)
-        wgrad[:, head_cols] = total * (1.0 / TILE_TOK)
-        return carry
-
-    lax.fori_loop(0, heads, finish, 0)
+        wgrad[:, cols] = total * (1.0 / TILE_TOK)
+
+    for h in range(heads):
+        gain_row = gain[:, h * HEAD : (h + 1) * HEAD]
+        arrived = tx.at[h, pl.ds(0, peers * BLOCK)]
+        await_blocks(arrived, in_recv.at[2 * h])
+        prepare(h, gain_row)
+        await_blocks(arrived, in_recv.at[2 * h + 1])
+        if h > 0:
+            send_grads(h - 1, 0, n)
+        attend(h, gain_row, h == heads - 1)
+        halves = weight_term(h)
+        if h > 0:
+            finish(h - 1)
+        send_sums(h, halves)
+    finish(heads - 1)
 
     for h in range(heads):
         sent = tx.at[h, pl.ds(0, peers * BLOCK)]
@@ -447,9 +458,8 @@
         await_blocks(sum_in.at[h], sum_send.at[h])
         await_blocks(sent, grad_send.at[h])
         await_blocks(sent, grad_recv.at[h])
-        pltpu.make_async_copy(
-            send_block.at[h, 0], send_block.at[h, 0], block_sem.at[h]
-        ).wait()
+        own_block = send_block.at[h, pl.ds(0, BLOCK)]
+        await_blocks(own_block, block_sem.at[h])
     for group in copies:
         for copy in group:
             copy.wait_send()
@@ -465,6 +475,7 @@
     out_rows = depth // enc
     tile_rows = feat.shape[1] * n
     anywhere = pl.BlockSpec(memory_space=pl.ANY)
+    hbm = pl.BlockSpec(memory_space=pltpu.HBM)
     vmem = pl.BlockSpec(memory_space=pltpu.VMEM)
     smem = pl.BlockSpec(memory_space=pltpu.SMEM)
     dma = pltpu.SemaphoreType.DMA
@@ -475,7 +486,7 @@
             jax.ShapeDtypeStruct(text.shape, BF16),
             jax.ShapeDtypeStruct((out_rows, heads * HEAD), F32),
         ),
-        in_specs=[anywhere] * 4 + [vmem, smem, smem, vmem],
+        in_specs=[hbm] * 5 + [smem, smem, hbm],
         out_specs=(anywhere, vmem),
         scratch_shapes=[
             pltpu.VMEM((tile_rows, depth), BF16),
@@ -483,20 +494,24 @@
             pltpu.VMEM((depth, heads * HEAD), BF16),
             pltpu.VMEM((tile_rows, heads * HEAD), BF16),
             pltpu.VMEM((heads, length, HEAD), BF16),
-            pltpu.VMEM((heads, n, 2 * BLOCK, HEAD), BF16),
+            pltpu.VMEM((heads, length, HEAD), BF16),
+            pltpu.VMEM((length, HEAD), BF16),
             pltpu.VMEM((length, HEAD), BF16),
             pltpu.VMEM((HEAD, length), BF16),
             pltpu.VMEM((length, HEAD), F32),
-            pltpu.VMEM((REACH + BLOCK, 2 * BLOCK), BF16),
+            pltpu.VMEM((2, REACH + GROUP, GROUP), BF16),
+            pltpu.VMEM((2, REACH + GROUP, GROUP), BF16),
             pltpu.VMEM((tile_rows, HEAD), BF16),
-            pltpu.VMEM((heads, n, BLOCK, HEAD), BF16),
+            pltpu.VMEM((heads, length, HEAD), BF16),
+            pltpu.VMEM((1, heads * HEAD), F32),
+            pltpu.VMEM((1, length), jnp.int32),
             pltpu.VMEM((1, length), jnp.int32),
             pltpu.VMEM((chips, out_rows, HEAD), F32),
             pltpu.VMEM((heads, chips, out_rows, HEAD), BF16),
             pltpu.VMEM((heads, chips, out_rows, HEAD), BF16),
             pltpu.VMEM((heads, chips, out_rows, HEAD), BF16),
             pltpu.VMEM((heads, chips - 1, out_rows, HEAD), BF16),
-            dma((2 + 2 * heads,)),
+            dma((4 + 2 * heads,)),
             dma((ring_copies,)),
             dma((ring_copies,)),
             dma((2 * heads,)),
@@ -510,7 +525,7 @@
             dma((heads,)),
         ],
         compiler_params=pltpu.CompilerParams(
-            collective_id=0, has_side_effects=True, vmem_limit_bytes=48 * 2**20
+            collective_id=0, has_side_effects=True, vmem_limit_bytes=60 * 2**20
         ),
     )(feat, weight, text, cot, gain.reshape(1, -1), count, slot, doc)
 

time: 132 us -> 110 us (0.83); the launches traced: 130 us -> 110 us
  Pallas kernels: 121 us -> 105 us
  local copies, waits for them, and re-layouts: 7.63 us -> 2.96 us
    pallas_call x1, Pallas kernels: 121 us -> 105 us  [per_device(): pl.pallas_call(functools.partial(whole_kernel, n, heads, enc), out_shape=...]
    unnamed x14 -> x4, local copies, waits for them, and re-layouts: 7.63 us -> 2.96 us
where the time goes in v2:
time: 110 us
  Pallas kernels  105 us (95%)
  local copies, waits for them, and re-layouts  2.96 us (3%)
  between operations  1.94 us (2%)
    pallas_call x1, Pallas kernels, per_device(): pl.pallas_call(functools.partial(whole_kernel, n, heads, enc), out_shape=...  105 us
    unnamed x4, local copies, waits for them, and re-layouts  2.96 us

profile of v2, /device:TPU:1, one launch (start us, length us, event | category | flops | bytes accessed | tf_op | source)
XLA Modules:
  0.0 110.1 jit_solution(17336964175231156306)
XLA Ops:
  1.9 105.2 %shard_map.95 = (bf16[1,128,4096]{2,1,0:T(8,128)(2,1)}, f32[80,256]{1,0:T(8,128)}) custom-call(bf16[1,16,2560]{2,1,0:T(8,128)(2,1)} %feat.1, bf16[2560,256]{1,0:T(8,128)(2,1)} %weight.1, bf16[1,128,4096]{2,1,0:T(8,128)(2,1)} %text.1, bf16[1,128,4096]{2,1,0:T(8,128)(2,1)} %cot.1, f32[1,256]{1,0:T(1,128)} %bitcast.1, s32[1]{0:T(128)S(6)} %copy.12.count, ...), custom_call_target="tpu_custom_call" | custom-call | tf_op jit(solution)/shard_map/pallas_call | solution.py:483
  107.1 0.0 copy-start
  107.2 2.3 %copy.14 = bf16[1,128,4096]{2,1,0:T(8,128)(2,1)} copy(bf16[1,128,4096]{2,1,0:T(8,128)(2,1)} %get-tuple-element.4) | data formatting | bytes 2097152
  109.5 0.0 copy-done
  109.5 0.6 copy.15
Async XLA Ops:
  107.1 2.3 %copy-start = (f32[80,256]{1,0:T(8,128)S(1)}, f32[80,256]{1,0:T(8,128)}, u32[]{:S(2)}) copy-start(f32[80,256]{1,0:T(8,128)} %get-tuple-element.5) | copy-start | bytes 245764

commit v3 on v2

--- a/solution.py
+++ b/solution.py
@@ -89,8 +89,29 @@
     def along(step):
         return lax.rem(me + 2 * step + 2 * n, n)
 
+    def partner(step):
+        away = n // 2 - lax.div(step + 1, 2)
+        return lax.rem(me + n + away * (1 - 2 * lax.rem(step, 2)), n)
+
     def rows(index, size):
         return pl.ds(pl.multiple_of(index * size, size), size)
+
+    barrier = pltpu.get_barrier_semaphore()
+
+    def greet_seq(d, carry):
+        pl.semaphore_signal(
+            barrier, inc=1, device_id=seq_id(lax.rem(me + d, n)), device_id_type=MESH
+        )
+        return carry
+
+    def greet_enc(d, carry):
+        to = 2 * lax.rem(chip + d, chips) + core
+        pl.semaphore_signal(barrier, inc=1, device_id=(to, me), device_id_type=MESH)
+        return carry
+
+    lax.fori_loop(1, n, greet_seq, 0)
+    lax.fori_loop(1, chips, greet_enc, 0)
+    pl.semaphore_signal(barrier, inc=1, device_id=(other_core, me), device_id_type=MESH)
 
     weight_copy = pltpu.make_async_copy(weight, wv, local_sem.at[0])
     weight_copy.start()
@@ -120,22 +141,6 @@
     doc_copy = pltpu.make_async_copy(doc_in, doc, local_sem.at[3 + 2 * heads])
     doc_copy.start()
 
-    barrier = pltpu.get_barrier_semaphore()
-
-    def greet_seq(d, carry):
-        pl.semaphore_signal(
-            barrier, inc=1, device_id=seq_id(lax.rem(me + d, n)), device_id_type=MESH
-        )
-        return carry
-
-    def greet_enc(d, carry):
-        to = 2 * lax.rem(chip + d, chips) + core
-        pl.semaphore_signal(barrier, inc=1, device_id=(to, me), device_id_type=MESH)
-        return carry
-
-    lax.fori_loop(1, n, greet_seq, 0)
-    lax.fori_loop(1, chips, greet_enc, 0)
-    pl.semaphore_signal(barrier, inc=1, device_id=(other_core, me), device_id_type=MESH)
     pl.semaphore_wait(barrier, peers + chips)
 
     def pass_on(source, index, to, number, first_col=0, cols=depth):
@@ -156,8 +161,8 @@
     half = depth // 2
 
     def exchange(h, source, to_cot, begin, end):
-        def body(d, carry):
-            to = lax.rem(me + d, n)
+        def body(step, carry):
+            to = partner(step)
             cols = pl.ds(pl.multiple_of(to * columns + h * HEAD, HEAD), HEAD)
             place = (ct if to_cot else tx).at[h, rows(me, BLOCK)]
             pltpu.make_async_remote_copy(
@@ -173,8 +178,8 @@
         lax.fori_loop(begin, end, body, 0)
 
     def exchange_part(h, part, parts):
-        begin = 1 + peers * part // parts
-        end = 1 + peers * (part + 1) // parts
+        begin = peers * part // parts
+        end = peers * (part + 1) // parts
         exchange(h, text, 0, begin, end)
         exchange(h, cot, 1, begin, end)
 
@@ -332,45 +337,47 @@
         send_block[h, here, :] = jnp.where(of_tile, 0.0, low).astype(BF16)
         image[...] = jnp.where(of_tile, low, image[...].astype(F32)).astype(BF16)
 
-    def send_grad(h, block):
-        source = send_block.at[h, rows(block, BLOCK)]
+    def send_grads(h, least, most):
         target = out.at[
             0, :, pl.ds(pl.multiple_of(me * columns + h * HEAD, HEAD), HEAD)
         ]
 
-        @pl.when(me == block)
+        def body(step, carry):
+            to = partner(step)
+
+            @pl.when((to >= least) & (to < most))
+            def _():
+                pltpu.make_async_remote_copy(
+                    src_ref=send_block.at[h, rows(to, BLOCK)],
+                    dst_ref=target,
+                    send_sem=grad_send.at[h],
+                    recv_sem=grad_recv.at[h],
+                    device_id=seq_id(to),
+                    device_id_type=MESH,
+                ).start()
+
+            return carry
+
+        lax.fori_loop(0, peers, body, 0)
+
+        @pl.when((me >= least) & (me < most))
         def _():
-            pltpu.make_async_copy(source, target, block_sem.at[h]).start()
-
-        @pl.when(me != block)
-        def _():
-            pltpu.make_async_remote_copy(
-                src_ref=source,
-                dst_ref=target,
-                send_sem=grad_send.at[h],
-                recv_sem=grad_recv.at[h],
-                device_id=seq_id(block),
-                device_id_type=MESH,
+            pltpu.make_async_copy(
+                send_block.at[h, rows(me, BLOCK)], target, block_sem.at[h]
             ).start()
 
-    def send_grads(h, begin, end):
-        def body(step, carry):
-            send_grad(h, end - 1 - step)
-            return carry
-
-        lax.fori_loop(0, end - begin, body, 0)
-
-    def attend(h, gain_row, at_once):
+    def attend(h, gain_row):
         dkv[...] = jnp.zeros_like(dkv)
         image[...] = jnp.zeros_like(image)
-        blocks = GROUP // BLOCK
         for index in range(groups - 1, -2, -1):
             if index >= 0:
                 score_part(h, index)
             if index < groups - 1:
                 product_part(h, index + 1, gain_row)
-                if at_once:
-                    send_grads(h, (index + 1) * blocks, (index + 2) * blocks)
+            if index in (groups // 2 - 1, -1):
+                done = (index + 1) * GROUP // BLOCK
+                if h == heads - 1:
+                    send_grads(h, done, done + n // 2)
 
     def weight_term(h):
         tile_grad = image[...]
@@ -444,7 +451,7 @@
         await_blocks(arrived, in_recv.at[2 * h + 1])
         if h > 0:
             send_grads(h - 1, 0, n)
-        attend(h, gain_row, h == heads - 1)
+        attend(h, gain_row)
         halves = weight_term(h)
         if h > 0:
             finish(h - 1)

time: 110 us -> 102 us (0.927)
  Pallas kernels: 105 us -> 96.6 us
    pallas_call x1, Pallas kernels: 105 us -> 96.6 us  [per_device(): pl.pallas_call(functools.partial(whole_kernel, n, heads, enc), out_shape=...]
where the time goes in v3:
time: 102 us
  Pallas kernels  96.6 us (95%)
  local copies, waits for them, and re-layouts  2.96 us (3%)
  between operations  1.94 us (2%)
    pallas_call x1, Pallas kernels, per_device(): pl.pallas_call(functools.partial(whole_kernel, n, heads, enc), out_shape=...  96.6 us
    unnamed x4, local copies, waits for them, and re-layouts  2.96 us

profile of v3, /device:TPU:1, one launch (start us, length us, event | category | flops | bytes accessed | tf_op | source)
XLA Modules:
  0.0 101.5 jit_solution(7757373272645791906)
XLA Ops:
  1.9 96.6 %shard_map.95 = (bf16[1,128,4096]{2,1,0:T(8,128)(2,1)}, f32[80,256]{1,0:T(8,128)}) custom-call(bf16[1,16,2560]{2,1,0:T(8,128)(2,1)} %feat.1, bf16[2560,256]{1,0:T(8,128)(2,1)} %weight.1, bf16[1,128,4096]{2,1,0:T(8,128)(2,1)} %text.1, bf16[1,128,4096]{2,1,0:T(8,128)(2,1)} %cot.1, f32[1,256]{1,0:T(1,128)} %bitcast.1, s32[1]{0:T(128)S(6)} %copy.12.count, ...), custom_call_target="tpu_custom_call" | custom-call | tf_op jit(solution)/shard_map/pallas_call | solution.py:490
  98.5 0.0 copy-start
  98.5 2.3 %copy.14 = bf16[1,128,4096]{2,1,0:T(8,128)(2,1)} copy(bf16[1,128,4096]{2,1,0:T(8,128)(2,1)} %get-tuple-element.4) | data formatting | bytes 2097152
  100.9 0.0 copy-done
  100.9 0.6 copy.15
Async XLA Ops:
  98.5 2.3 %copy-start = (f32[80,256]{1,0:T(8,128)S(1)}, f32[80,256]{1,0:T(8,128)}, u32[]{:S(2)}) copy-start(f32[80,256]{1,0:T(8,128)} %get-tuple-element.5) | copy-start | bytes 245764

commit v4 on v3

--- a/solution.py
+++ b/solution.py
@@ -490,8 +490,8 @@
     return pl.pallas_call(
         functools.partial(whole_kernel, n, heads, enc),
         out_shape=(
-            jax.ShapeDtypeStruct(text.shape, BF16),
-            jax.ShapeDtypeStruct((out_rows, heads * HEAD), F32),
+            pltpu.VMEM(text.shape, BF16),
+            pltpu.VMEM((out_rows, heads * HEAD), F32),
         ),
         in_specs=[hbm] * 5 + [smem, smem, hbm],
         out_specs=(anywhere, vmem),
@@ -532,7 +532,7 @@
             dma((heads,)),
         ],
         compiler_params=pltpu.CompilerParams(
-            collective_id=0, has_side_effects=True, vmem_limit_bytes=60 * 2**20
+            collective_id=0, has_side_effects=True, vmem_limit_bytes=56 * 2**20
         ),
     )(feat, weight, text, cot, gain.reshape(1, -1), count, slot, doc)
 

time: 102 us -> 99.6 us (0.976)
  local copies, waits for them, and re-layouts: 2.96 us -> 1.61 us
    unnamed x4 -> x2, local copies, waits for them, and re-layouts: 2.96 us -> 1.61 us
where the time goes in v4:
time: 99.6 us; the launch traced here: 99.4 us
  Pallas kernels  95.9 us (96%)
  between operations  1.93 us (2%)
  local copies, waits for them, and re-layouts  1.61 us (2%)
    pallas_call x1, Pallas kernels, per_device(): pl.pallas_call(functools.partial(whole_kernel, n, heads, enc), out_shape=...  95.9 us

profile of v4, /device:TPU:1, one launch (start us, length us, event | category | flops | bytes accessed | tf_op | source)
XLA Modules:
  0.0 99.4 jit_solution(11481587602582935596)
XLA Ops:
  1.9 95.9 %shard_map.95 = (bf16[1,128,4096]{2,1,0:T(8,128)(2,1)S(1)}, f32[80,256]{1,0:T(8,128)S(1)}) custom-call(bf16[1,16,2560]{2,1,0:T(8,128)(2,1)} %feat.1, bf16[2560,256]{1,0:T(8,128)(2,1)} %weight.1, bf16[1,128,4096]{2,1,0:T(8,128)(2,1)} %text.1, bf16[1,128,4096]{2,1,0:T(8,128)(2,1)} %cot.1, f32[1,256]{1,0:T(1,128)} %bitcast.1, s32[1]{0:T(128)S(6)} %copy.14.count, ...), custom_call_target="tpu_custom_call" | custom-call | tf_op jit(solution)/shard_map/pallas_call | solution.py:490
  97.8 1.0 copy.12
  98.8 0.6 copy.13

commit v5 on v4

--- a/solution.py
+++ b/solution.py
@@ -216,7 +216,7 @@
     ]
     for copy in [right, left] + sideways:
         copy.start()
-    exchange_part(0, parts - 1, parts)
+    exchange_part(0, full_steps, parts)
     right.wait_recv()
     left.wait_recv()
     farthest = pass_on(None, along(ring // 2), beside, x_base + 2 * last + 1)
@@ -382,22 +382,21 @@
     def weight_term(h):
         tile_grad = image[...]
 
-        def weight_rows(index, carry):
-            mine = pl.multiple_of((2 * index + core) * out_rows, out_rows)
-            theirs = pl.multiple_of((2 * index + 1 - core) * out_rows, out_rows)
-            half_out[h, index] = jnp.dot(
-                featT[pl.ds(theirs, out_rows), :],
-                tile_grad,
-                preferred_element_type=F32,
-            ).astype(BF16)
-            keep[index] = jnp.dot(
-                featT[pl.ds(mine, out_rows), :],
-                tile_grad,
-                preferred_element_type=F32,
+        def block_of_rows(index, of_core):
+            place = pl.multiple_of((2 * index + of_core) * out_rows, out_rows)
+            return jnp.dot(
+                featT[pl.ds(place, out_rows), :], tile_grad, preferred_element_type=F32
             )
+
+        def theirs(index, carry):
+            half_out[h, index] = block_of_rows(index, 1 - core).astype(BF16)
             return carry
 
-        lax.fori_loop(0, chips, weight_rows, 0)
+        def mine(index, carry):
+            keep[index] = block_of_rows(index, core)
+            return carry
+
+        lax.fori_loop(0, chips, theirs, 0)
         halves = pltpu.make_async_remote_copy(
             src_ref=half_out.at[h],
             dst_ref=half_in.at[h],
@@ -407,22 +406,18 @@
             device_id_type=MESH,
         )
         halves.start()
+        lax.fori_loop(0, chips, mine, 0)
         return halves
 
     def send_sums(h, halves):
         halves.wait()
 
-        def add_halves(index, carry):
-            value = keep[index] + half_in[h, index].astype(F32)
-            keep[index] = value
-            sum_out[h, index] = value.astype(BF16)
-            return carry
-
-        lax.fori_loop(0, chips, add_halves, 0)
-        wgrad[:, h * HEAD : (h + 1) * HEAD] = keep[chip]
+        wgrad[:, h * HEAD : (h + 1) * HEAD] = keep[chip] + half_in[h, chip].astype(F32)
 
         def body(d, carry):
             to = lax.rem(chip + d, chips)
+            value = keep[to] + half_in[h, to].astype(F32)
+            sum_out[h, to] = value.astype(BF16)
             pltpu.make_async_remote_copy(
                 src_ref=sum_out.at[h, to],
                 dst_ref=sum_in.at[h, d - 1],

time: 99.6 us -> 99.2 us (level)
  no operation moved by 1% of the time
where the time goes in v5:
time: 99.2 us; the launch traced here: 98.8 us
  Pallas kernels  95.2 us (96%)
  between operations  1.93 us (2%)
  local copies, waits for them, and re-layouts  1.61 us (2%)
    pallas_call x1, Pallas kernels, per_device(): pl.pallas_call(functools.partial(whole_kernel, n, heads, enc), out_shape=...  95.2 us

profile of v5, /device:TPU:1, one launch (start us, length us, event | category | flops | bytes accessed | tf_op | source)
XLA Modules:
  0.0 98.8 jit_solution(5240575866375075180)
XLA Ops:
  1.9 95.2 %shard_map.95 = (bf16[1,128,4096]{2,1,0:T(8,128)(2,1)S(1)}, f32[80,256]{1,0:T(8,128)S(1)}) custom-call(bf16[1,16,2560]{2,1,0:T(8,128)(2,1)} %feat.1, bf16[2560,256]{1,0:T(8,128)(2,1)} %weight.1, bf16[1,128,4096]{2,1,0:T(8,128)(2,1)} %text.1, bf16[1,128,4096]{2,1,0:T(8,128)(2,1)} %cot.1, f32[1,256]{1,0:T(1,128)} %bitcast.1, s32[1]{0:T(128)S(6)} %copy.14.count, ...), custom_call_target="tpu_custom_call" | custom-call | tf_op jit(solution)/shard_map/pallas_call | solution.py:485
  97.2 1.0 copy.12
  98.1 0.6 copy.13
